TPU v7x, 32 devices: a whole 2x2x4 slice. The times are simulated.
32 devices in a mesh: dp: 8 (over y, x, core), node: 4 (over z).
Axes of the slice: x: 2, y: 2, z: 4, core: 2. Of those that a mesh axis runs over, the one named last changes fastest.
Arguments:
- tokens: bfloat16 [16384, 8192], P(('dp', 'node')), may hold values from -6 to 6
- weight_codes: bfloat16 [8192, 1024], P('node'), may hold values from -4 to 4
- block_scales: float32 [64, 8], P('node'), may hold values from 0.0055242716 to 0.022097087
- value_grad: bfloat16 [16384, 1024], P(('dp', 'node')), may hold values from -6 to 6
Outputs:
- values: bfloat16 [16384, 1024], P(('dp', 'node'))
- input_grad: bfloat16 [16384, 8192], P(('dp', 'node'))
- weight_grad: float32 [8192, 1024], P(('dp', 'node'))
All inputs are finite; a program needn't handle non-finite values.
Results may differ from a plain program's by a relative error of at most 0.0055.
Values may be sent and summed in bfloat16 or wider, within the bound.
A program may use at most 192 MiB of HBM per device.

v0:
```python
import jax
import jax.numpy as jnp
from jax import lax
from jax.sharding import PartitionSpec as P


def shards(tokens, weight_codes, block_scales, value_grad):
    row_count, col_count = weight_codes.shape
    row_blocks, col_blocks = block_scales.shape
    scaled = (
        weight_codes.astype(jnp.float32).reshape(
            row_blocks, row_count // row_blocks, col_blocks, col_count // col_blocks
        )
        * block_scales[:, None, :, None]
    )
    local_weight = scaled.reshape(row_count, col_count).astype(jnp.bfloat16)
    full_weight = lax.all_gather(local_weight, "node", axis=0, tiled=True)
    values = jnp.dot(tokens, full_weight, preferred_element_type=jnp.float32).astype(jnp.bfloat16)
    input_grad = lax.dot_general(
        value_grad, full_weight, (((1,), (1,)), ((), ())), preferred_element_type=jnp.float32
    ).astype(jnp.bfloat16)
    data_count = lax.axis_size("dp")
    node_count = lax.axis_size("node")
    total_tokens = tokens.shape[0] * data_count * node_count
    product = lax.dot_general(
        tokens, value_grad, (((0,), (0,)), ((), ())), preferred_element_type=jnp.float32
    )
    grad_term = (product * total_tokens ** (-0.5)).astype(jnp.bfloat16)
    first_hop = lax.all_to_all(grad_term[None], "dp", split_axis=1, concat_axis=0, tiled=True)
    partial_value = jnp.sum(first_hop, axis=0, dtype=jnp.float32)
    second_hop = lax.all_to_all(
        partial_value[None].astype(jnp.bfloat16), "node", split_axis=1, concat_axis=0, tiled=True
    ).astype(jnp.float32)
    weight_grad = jnp.sum(second_hop, axis=0)
    return (values, input_grad, weight_grad)


def solution(mesh):
    in_specs = (P(("dp", "node"), None), P("node", None), P("node", None), P(("dp", "node"), None))
    out_specs = (P(("dp", "node"), None), P(("dp", "node"), None), P(("dp", "node"), None))
    return jax.shard_map(shards, mesh=mesh, in_specs=in_specs, out_specs=out_specs, check_vma=False)
```

profile of v0, /device:TPU:0, one launch (start us, length us, event | category | flops | bytes accessed | tf_op | source)
XLA Modules:
  0.0 560.1 jit_solution(8693495403516455557)
XLA Ops:
  7.2 0.8 copy.14
  8.1 0.6 mul.17
  8.7 1.6 copy-done.1
  10.3 4.2 fusion.2
  14.5 16.8 %fusion = bf16[1,8192,1024]{2,1,0:T(8,128)(2,1)} fusion(bf16[512,8192]{1,0:T(8,128)(2,1)} %param.4, bf16[512,1024]{1,0:T(8,128)(2,1)S(1)} %copy-done), kind=kOutput, calls=%fused_computation.1 | convolution fusion | flops 8606711808 | bytes 26214400 | tf_op jit(solution)/shard_map/dot_general | solution.py:25
  31.3 29.2 %copy.25 = bf16[1,8192,1024]{2,0,1:T(2,128)(2,1)} copy(bf16[1,8192,1024]{2,1,0:T(8,128)(2,1)} %fusion) | data formatting | bytes 33554432 | tf_op jit(solution)/shard_map/broadcast_in_dim | solution.py:29
  60.4 0.5 broadcast.2
  61.0 96.6 %reduce.1 = bf16[8192,1024]{1,0:T(8,128)(2,1)} reduce(bf16[8192,1,1024]{2,1,0:T(2,128)(2,1)} %bitcast.29, bf16[]{:T(256)} %broadcast.2), dimensions={1}, to_apply=%bitcast.27.reduce_sub_computation | reduce | bytes 33554432
  157.6 18.0 %reshape.30 = bf16[8,2,524288]{2,1,0:T(2,128)(2,1)} reshape(bf16[8192,1024]{1,0:T(8,128)(2,1)} %reduce.1) | data formatting | bytes 33554432
  175.6 192.1 %all_to_all.8 = bf16[8,2,524288]{2,1,0:T(2,128)(2,1)} all-to-all(bf16[8,2,524288]{2,1,0:T(2,128)(2,1)} %reshape.30), channel_id=1, replica_groups=mesh['dp'=8,'node'=4] {'dp'}, dimensions={0} | all-to-all | bytes 33554432 | tf_op jit(solution)/shard_map/all_to_all | solution.py:29
  367.7 22.3 %reshape.31 = bf16[8192,1,1024]{2,1,0:T(2,128)(2,1)} reshape(bf16[8,2,524288]{2,1,0:T(2,128)(2,1)} %all_to_all.8) | data formatting | bytes 33554432
  390.0 21.9 %copy.19 = bf16[1,8192,1024]{2,1,0:T(8,128)(2,1)} copy(bf16[1,8192,1024]{2,0,1:T(2,128)(2,1)} %bitcast.30) | data formatting | bytes 33554432
  411.9 9.5 %reduce = bf16[1024,1024]{1,0:T(8,128)(2,1)S(1)} reduce(bf16[8,1024,1024]{2,1,0:T(8,128)(2,1)} %bitcast.31, bf16[]{:T(256)} %constant.4), dimensions={0}, to_apply=%region_0.0.clone | reduce | flops 7340032 | bytes 18874370 | tf_op jit(solution)/shard_map/reduce_sum | solution.py:30
  421.4 5.2 copy.26
  426.6 12.8 %reduce.2 = bf16[1024,1024]{1,0:T(8,128)(2,1)S(1)} reduce(bf16[1024,1,1024]{2,1,0:T(2,128)(2,1)} %bitcast.33, bf16[]{:T(256)} %broadcast.2), dimensions={1}, to_apply=%bitcast.28.reduce_sub_computation | reduce | bytes 4194306
  439.3 2.8 reshape.32
  442.1 53.4 %all_to_all.9 = bf16[4,2,131072]{2,1,0:T(2,128)(2,1)S(1)} all-to-all(bf16[4,2,131072]{2,1,0:T(2,128)(2,1)} %reshape.32), channel_id=1, replica_groups=mesh['dp'=8,'node'=4] {'node'}, dimensions={0} | all-to-all | bytes 4194304 | tf_op jit(solution)/shard_map/all_to_all | solution.py:31
  495.5 3.4 reshape.33
  498.9 5.2 copy.20
  504.0 3.7 reduce_sum.19
  507.7 16.9 %fusion.1 = bf16[512,8192]{0,1:T(8,128)(2,1)} fusion(bf16[8192,1024]{1,0:T(8,128)(2,1)} %all-gather.2.cloned.1.call-done, bf16[512,1024]{1,0:T(8,128)(2,1)S(1)} %copy-done), kind=kOutput, calls=%fused_computation.3 | convolution fusion | flops 8594128896 | bytes 26214400 | tf_op jit(solution)/shard_map/dot_general | solution.py:19
  524.7 11.9 %copy.18 = bf16[512,8192]{1,0:T(8,128)(2,1)} copy(bf16[512,8192]{0,1:T(8,128)(2,1)} %fusion.1) | data formatting | bytes 16777216
  536.6 14.9 %fusion.3 = bf16[512,1024]{0,1:T(8,128)(2,1)S(1)} fusion(bf16[8192,1024]{1,0:T(8,128)(2,1)} %all-gather.2.cloned.1.call-done, bf16[512,8192]{1,0:T(8,128)(2,1)} %param.4), kind=kOutput, calls=%fused_computation.7 | convolution fusion | flops 8590458880 | bytes 26214400 | tf_op jit(solution)/shard_map/dot_general | solution.py:18
  551.5 1.3 copy.17
  (6 shorter events, 0.1 us)
Async XLA Ops:
  7.2 7.3 %copy-start = (bf16[512,1024]{1,0:T(8,128)(2,1)S(1)}, bf16[512,1024]{1,0:T(8,128)(2,1)}, u32[]{:S(2)}) copy-start(bf16[512,1024]{1,0:T(8,128)(2,1)} %param.7) | copy-start | bytes 3145732
  7.2 500.6 %all-gather.2.cloned.1.call-start = ((), (), s32[]{:S(2)}) async-start(), calls=%async_computation.2 | async-start | bytes 20971520 | tf_op jit(solution)/shard_map/all_gather | solution.py:17
  8.1 2.2 copy-start.1
Sparse Core Ops, SparseCore 0:
  14.6 289.4 all-gather.1
where the time goes:
time: 564 us; the launch traced here: 560 us
  blocking collectives  245 us (43%)
  other arithmetic  127 us (23%)
  local copies, waits for them, and re-layouts  125 us (22%)
  matrix products  48.6 us (9%)
  between operations  14.5 us (3%)
    all_to_all x1, blocking collectives, shards(): lax.all_to_all(grad_term[None], 'dp', split_axis=1, concat_axis=0, tiled=...  192 us
    unnamed x2, other arithmetic  109 us
    unnamed x14, local copies, waits for them, and re-layouts  89.7 us
    all_to_all x1, blocking collectives, shards(): lax.all_to_all(partial_value[None].astype(jnp.bfloat16), 'node', split_ax...  53.4 us
    broadcast_in_dim x1, local copies, waits for them, and re-layouts, shards(): grad_term[None]  29.2 us
    dot_general x1, matrix products, shards(): lax.dot_general(value_grad, full_weight, (((1,), (1,)), ((), ())), prefer...  16.9 us
    dot_general x1, matrix products, shards(): lax.dot_general(tokens, value_grad, (((0,), (0,)), ((), ())), preferred_e...  16.8 us
    dot_general x1, matrix products, shards(): jnp.dot(tokens, full_weight, preferred_element_type=jnp.float32)  14.9 us
  transfers between devices with their start and end apart: 1, of which 0 were waited for; matrix products, arithmetic and copies ran while one was open for 44% of the time, Pallas kernels for 0%

commit v1 on v0

v1 whole, which is shorter than its diff:
```python
import jax
import jax.numpy as jnp
from jax import lax
from jax.sharding import PartitionSpec as P


def dequantized(weight_codes, block_scales):
    row_count, col_count = weight_codes.shape
    row_blocks, col_blocks = block_scales.shape
    scaled = (
        weight_codes.astype(jnp.float32).reshape(
            row_blocks, row_count // row_blocks, col_blocks, col_count // col_blocks
        )
        * block_scales[:, None, :, None]
    )
    return scaled.reshape(row_count, col_count).astype(jnp.bfloat16)


def scattered_sum(term, data_count, node_count, chunk_count):
    data_index = lax.axis_index("dp")
    node_index = lax.axis_index("node")
    bits = data_count.bit_length() - 1
    width = term.shape[1] // chunk_count
    rows = term.shape[0] // (data_count * node_count)
    sums = []
    for chunk in range(chunk_count):
        block = term[:, chunk * width:(chunk + 1) * width]
        order = list(range(1, bits))
        turn = chunk % len(order) if order else 0
        order = list(range(min(bits, 1))) + order[turn:] + order[:turn]
        left = list(range(bits))
        for bit in order:
            stride = 1 << bit
            pairs = [(i, i ^ stride) for i in range(data_count)]
            mine = (data_index // stride) % 2
            inner = rows * node_count << sum(1 for other in left if other < bit)
            view = block.reshape(-1, 2, inner, width)
            going = lax.dynamic_index_in_dim(view, 1 - mine, 1, keepdims=False)
            kept = lax.dynamic_index_in_dim(view, mine, 1, keepdims=False)
            came = lax.ppermute(going, "dp", pairs)
            block = (kept.astype(jnp.float32) + came.astype(jnp.float32)).astype(jnp.bfloat16)
            left.remove(bit)
        view = block.reshape(node_count, rows, width)
        total = lax.dynamic_index_in_dim(view, node_index, 0, keepdims=False).astype(jnp.float32)
        for shift in range(1, node_count):
            target = (node_index + shift) % node_count
            going = lax.dynamic_index_in_dim(view, target, 0, keepdims=False)
            pairs = [(i, (i + shift) % node_count) for i in range(node_count)]
            total = total + lax.ppermute(going, "node", pairs).astype(jnp.float32)
        sums.append(total)
    return jnp.concatenate(sums, axis=1)


def whole_weight(local_weight, data_count, node_count, part_count):
    data_index = lax.axis_index("dp")
    node_index = lax.axis_index("node")
    bits = data_count.bit_length() - 1
    rows = local_weight.shape[0] // data_count
    width = local_weight.shape[1] // part_count
    piece = lax.dynamic_slice_in_dim(local_weight, data_index * rows, rows, 0)
    parts = []
    for part in range(part_count):
        own = piece[:, part * width:(part + 1) * width]
        held = jnp.zeros((node_count, rows, width), local_weight.dtype)
        held = lax.dynamic_update_index_in_dim(held, own, node_index, 0)
        for shift in range(1, node_count):
            pairs = [(i, (i + shift) % node_count) for i in range(node_count)]
            came = lax.ppermute(own, "node", pairs)
            held = lax.dynamic_update_index_in_dim(held, came, (node_index - shift) % node_count, 0)
        order = list(range(1, bits))
        turn = part % len(order) if order else 0
        order = order[turn:] + order[:turn] + list(range(min(bits, 1)))
        done = []
        block = held.reshape(node_count, 1, rows, width)
        for bit in order:
            stride = 1 << bit
            pairs = [(i, i ^ stride) for i in range(data_count)]
            mine = (data_index // stride) % 2
            came = lax.ppermute(block, "dp", pairs)
            low = sum(1 for other in done if other < bit)
            high = len(done) - low
            here = block.reshape(node_count, 1 << high, 1, (1 << low), rows, width)
            there = came.reshape(here.shape)
            first = jnp.where(mine == 0, here, there)
            second = jnp.where(mine == 0, there, here)
            block = jnp.concatenate([first, second], axis=2).reshape(node_count, -1, rows, width)
            done.append(bit)
        parts.append(block.reshape(-1, width))
    return jnp.concatenate(parts, axis=1)


def shards(tokens, weight_codes, block_scales, value_grad):
    data_count = lax.axis_size("dp")
    node_count = lax.axis_size("node")
    total_tokens = tokens.shape[0] * data_count * node_count
    local_weight = dequantized(weight_codes, block_scales)
    full_weight = whole_weight(local_weight, data_count, node_count, 2)
    product = lax.dot_general(
        tokens, value_grad, (((0,), (0,)), ((), ())), preferred_element_type=jnp.float32
    )
    grad_term = (product * total_tokens ** (-0.5)).astype(jnp.bfloat16)
    weight_grad = scattered_sum(grad_term, data_count, node_count, 2)
    values = jnp.dot(tokens, full_weight, preferred_element_type=jnp.float32).astype(jnp.bfloat16)
    input_grad = lax.dot_general(
        value_grad, full_weight, (((1,), (1,)), ((), ())), preferred_element_type=jnp.float32
    ).astype(jnp.bfloat16)
    return (values, input_grad, weight_grad)


def solution(mesh):
    in_specs = (P(("dp", "node"), None), P("node", None), P("node", None), P(("dp", "node"), None))
    out_specs = (P(("dp", "node"), None), P(("dp", "node"), None), P(("dp", "node"), None))
    return jax.shard_map(shards, mesh=mesh, in_specs=in_specs, out_specs=out_specs, check_vma=False)
```

time: 564 us -> 364 us (0.65)
  blocking collectives: 245 us -> 0 us
  waiting for transfers between devices: 0.02 us -> 126 us
  starting transfers between devices: 0.04 us -> 71.3 us
  other arithmetic: 127 us -> 56.7 us
  local copies, waits for them, and re-layouts: 125 us -> 63.7 us
  between operations: 14.5 us -> 1.07 us
    all_to_all x2 -> x0, blocking collectives: 245 us -> none  [the longest x1 192 us: shards(): lax.all_to_all(grad_term[None], 'dp', split_axis=1, concat_axis=0, tiled=...]
    ppermute x0 -> x24, waiting for transfers between devices: none -> 126 us  [the longest x6 49.5 us: scattered_sum(): came = lax.ppermute(going, 'dp', pairs)]
    unnamed x2 -> x1, other arithmetic: 109 us -> 0.01 us
    ppermute x0 -> x24, starting transfers between devices: none -> 71.3 us  [the longest x6 29.5 us: scattered_sum(): total = total + lax.ppermute(going, 'node', pairs).astype(jnp.float32)]
    unnamed x14 -> x44, local copies, waits for them, and re-layouts: 89.7 us -> 25.6 us
    broadcast_in_dim x1 -> x0, local copies, waits for them, and re-layouts: 29.2 us -> none  [shards(): grad_term[None]]
    select_n x0 -> x6, other arithmetic: none -> 17.3 us  [whole_weight(): first = jnp.where(mine == 0, here, there)]
    concatenate x0 -> x5, other arithmetic: none -> 16.5 us  [the longest x4 15.5 us: whole_weight(): jnp.concatenate([first, second], axis=2)]
  transfers between devices with their start and end apart: 1 -> 24, of which waited for: 0 -> 15; matrix products, arithmetic and copies ran while one was open for 44% -> 20% of each run, Pallas kernels for 0% -> 0%
where the time goes in v1:
time: 364 us; the launch traced here: 363 us
  waiting for transfers between devices  126 us (35%)
  starting transfers between devices  71.3 us (20%)
  local copies, waits for them, and re-layouts  63.7 us (18%)
  other arithmetic  56.7 us (16%)
  matrix products  44.4 us (12%)
    ppermute x6, waiting for transfers between devices, scattered_sum(): came = lax.ppermute(going, 'dp', pairs)  49.5 us
    ppermute x6, waiting for transfers between devices, whole_weight(): came = lax.ppermute(block, 'dp', pairs)  49.3 us
    ppermute x6, starting transfers between devices, scattered_sum(): total = total + lax.ppermute(going, 'node', pairs).astype(jnp.float32)  29.5 us
    ppermute x6, starting transfers between devices, whole_weight(): came = lax.ppermute(own, 'node', pairs)  29.5 us
    unnamed x44, local copies, waits for them, and re-layouts  25.6 us
    select_n x6, other arithmetic, whole_weight(): first = jnp.where(mine == 0, here, there)  17.3 us
    convert_element_type x6, other arithmetic, scattered_sum(): (kept.astype(jnp.float32) + came.astype(jnp.float32)).astype(jnp.bfloat16)  15.9 us
    dot_general x1, matrix products, shards(): lax.dot_general(tokens, value_grad, (((0,), (0,)), ((), ())), preferred_e...  15.9 us
  transfers between devices with their start and end apart: 24, of which 15 were waited for; matrix products, arithmetic and copies ran while one was open for 20% of the time, Pallas kernels for 0%

profile of v1, /device:TPU:0, one launch (start us, length us, event | category | flops | bytes accessed | tf_op | source)
XLA Modules:
  0.0 362.9 jit_solution(6311902805956416573)
XLA Ops:
  1.9 15.9 %multiply_convert_fusion = bf16[8192,1024]{1,0:T(8,128)(2,1)} fusion(bf16[512,8192]{1,0:T(8,128)(2,1)} %param.4, bf16[512,1024]{1,0:T(8,128)(2,1)S(1)} %copy-done), kind=kOutput, calls=%fused_computation | convolution fusion | flops 8606711808 | bytes 26214400 | tf_op jit(solution)/shard_map/dot_general | solution.py:98
  17.8 11.4 %fusion.20 = (bf16[8192,512]{1,0:T(8,128)(2,1)}, bf16[8192,512]{1,0:T(8,128)(2,1)}) fusion(bf16[8192,1024]{1,0:T(8,128)(2,1)} %multiply_convert_fusion), kind=kLoop, calls=%fused_computation.72 | loop fusion | bytes 33554432 | tf_op jit(solution)/shard_map/slice | solution.py:27
  29.1 4.8 %dynamic-slice_bitcast_fusion.1 = bf16[4,1024,512]{2,1,0:T(8,128)(2,1)} fusion(bf16[4,2,1024,512]{3,2,1,0:T(8,128)(2,1)} %bitcast.148, s32[]{:T(128)S(6)} %select_n.294), kind=kLoop, calls=%fused_computation.19 | loop fusion | bytes 8388612 | tf_op jit(solution)/shard_map/jit(dynamic_index_in_dim)/squeeze | solution.py:38
  38.8 5.5 %copy.23 = f32[256,8,8,128]{3,1,2,0:T(8,128)} copy(f32[256,8,8,128]{3,2,1,0:T(8,128)S(1)} %bitcast.143) | data formatting | bytes 16777216
  54.3 4.3 %collective-permute-done.6 = bf16[256,512]{1,0:T(8,128)(2,1)S(1)} collective-permute-done((bf16[256,512]{1,0:T(8,128)(2,1)}, bf16[256,512]{1,0:T(8,128)(2,1)S(1)}, u32[]{:S(2)}, u32[]{:S(2)}) %collective-permute-start.6) | collective-permute-done | bytes 262176 | tf_op jit(solution)/shard_map/ppermute | solution.py:68
  58.7 9.8 %collective-permute-start = (bf16[256,512]{1,0:T(8,128)(2,1)}, bf16[256,512]{1,0:T(8,128)(2,1)S(1)}, u32[]{:S(2)}, u32[]{:S(2)}) collective-permute-start(bf16[256,512]{1,0:T(8,128)(2,1)} %get-tuple-element.29), channel_id=1, source_target_pairs={{0,1},{1,2},{2,3},{3,0},{4,5},{5,6},{6,7},{7,4},{8,9},{9,10},{10,1... | collective-permute-start | bytes 786440 | tf_op jit(solution)/shard_map/ppermute | solution.py:68
  70.8 12.3 %collective-permute-start.2 = (bf16[256,512]{1,0:T(8,128)(2,1)}, bf16[256,512]{1,0:T(8,128)(2,1)S(1)}, u32[]{:S(2)}, u32[]{:S(2)}) collective-permute-start(bf16[256,512]{1,0:T(8,128)(2,1)} %get-tuple-element.29), channel_id=1, source_target_pairs={{0,3},{1,0},{2,1},{3,2},{4,7},{5,4},{6,5},{7,6},{8,11},{9,8},{10,9... | collective-permute-start | bytes 786440 | tf_op jit(solution)/shard_map/ppermute | solution.py:68
  85.5 6.8 %collective-permute-done.1 = bf16[256,512]{1,0:T(8,128)(2,1)S(1)} collective-permute-done((bf16[256,512]{1,0:T(8,128)(2,1)}, bf16[256,512]{1,0:T(8,128)(2,1)S(1)}, u32[]{:S(2)}, u32[]{:S(2)}) %collective-permute-start.1) | collective-permute-done | bytes 262176 | tf_op jit(solution)/shard_map/ppermute | solution.py:68
  97.8 5.9 %collective-permute-done.9 = bf16[4,1,256,512]{3,2,0,1:T(8,128)(2,1)} collective-permute-done((bf16[4,1,256,512]{3,2,0,1:T(8,128)(2,1)S(1)}, bf16[4,1,256,512]{3,2,0,1:T(8,128)(2,1)}, u32[]{:S(2)}, u32[]{:S(2)}) %collective-permute-start.9) | collective-permute-done | bytes 1048608 | tf_op jit(solution)/shard_map/ppermute | solution.py:79
  108.2 14.4 %collective-permute-done.3 = bf16[4,1,256,512]{3,2,0,1:T(8,128)(2,1)} collective-permute-done((bf16[4,1,256,512]{3,2,0,1:T(8,128)(2,1)}, bf16[4,1,256,512]{3,2,0,1:T(8,128)(2,1)}, u32[]{:S(2)}, u32[]{:S(2)}) %collective-permute-start.3) | collective-permute-done | bytes 1048608 | tf_op jit(solution)/shard_map/ppermute | solution.py:79
  128.8 4.8 %fusion.3 = bf16[4,1024,512]{2,1,0:T(8,128)(2,1)S(1)} fusion(bf16[4,1024,512]{2,1,0:T(8,128)(2,1)} %collective-permute-done.12, bf16[4,2,1024,512]{3,2,1,0:T(8,128)(2,1)} %bitcast.149, s32[]{:T(128)S(6)} %select_n.293), kind=kLoop, calls=%fused_computation.11 | loop fusion | flops 8388608 | bytes 12582916 | tf_op jit(solution)/shard_map/convert_element_type | solution.py:41
  142.9 24.7 %collective-permute-done.10 = bf16[4,2,256,512]{3,2,1,0:T(8,128)(2,1)} collective-permute-done((bf16[4,2,256,512]{3,2,1,0:T(8,128)(2,1)}, bf16[4,2,256,512]{3,2,1,0:T(8,128)(2,1)}, u32[]{:S(2)}, u32[]{:S(2)}) %collective-permute-start.10) | collective-permute-done | bytes 2097184 | tf_op jit(solution)/shard_map/ppermute | solution.py:79
  181.0 30.3 %collective-permute-done.13 = bf16[2,1024,512]{2,1,0:T(8,128)(2,1)} collective-permute-done((bf16[2,1024,512]{2,1,0:T(8,128)(2,1)}, bf16[2,1024,512]{2,1,0:T(8,128)(2,1)}, u32[]{:S(2)}, u32[]{:S(2)}) %collective-permute-start.13) | collective-permute-done | bytes 2097184 | tf_op jit(solution)/shard_map/ppermute | solution.py:40
  223.5 16.6 %collective-permute-done.14 = bf16[1,1024,512]{2,1,0:T(8,128)(2,1)} collective-permute-done((bf16[1,1024,512]{2,1,0:T(8,128)(2,1)}, bf16[1,1024,512]{2,1,0:T(8,128)(2,1)}, u32[]{:S(2)}, u32[]{:S(2)}) %collective-permute-start.14) | collective-permute-done | bytes 1048608 | tf_op jit(solution)/shard_map/ppermute | solution.py:40
  253.9 7.8 %collective-permute-start.21 = (bf16[256,512]{1,0:T(8,128)(2,1)S(1)}, bf16[256,512]{1,0:T(8,128)(2,1)S(1)}, u32[]{:S(2)}, u32[]{:S(2)}) collective-permute-start(bf16[256,512]{1,0:T(8,128)(2,1)S(1)} %get-tuple-element.26), channel_id=1, source_target_pairs={{0,1},{1,2},{2,3},{3,0},{4,5},{5,6},{6,7},{7,4},{8,9},{9,10},{10,1... | collective-permute-start | bytes 786440 | tf_op jit(solution)/shard_map/ppermute | solution.py:49
  266.5 15.5 %collective-permute-start.23 = (bf16[256,512]{1,0:T(8,128)(2,1)S(1)}, bf16[256,512]{1,0:T(8,128)(2,1)S(1)}, u32[]{:S(2)}, u32[]{:S(2)}) collective-permute-start(bf16[256,512]{1,0:T(8,128)(2,1)S(1)} %get-tuple-element.27), channel_id=1, source_target_pairs={{0,3},{1,0},{2,1},{3,2},{4,7},{5,4},{6,5},{7,6},{8,11},{9,8},{10,9... | collective-permute-start | bytes 786440 | tf_op jit(solution)/shard_map/ppermute | solution.py:49
  290.6 5.1 %select_bitcast_fusion.1 = (bf16[4,4,1,1,256,512]{5,4,1,0,3,2:T(8,128)(2,1)S(1)}, bf16[4,4,1,1,256,512]{5,4,1,0,3,2:T(8,128)(2,1)}) fusion(bf16[4,4,256,512]{3,2,1,0:T(8,128)(2,1)} %bitcast.29, bf16[4,4,256,512]{3,2,1,0:T(8,128)(2,1)} %collective-permute-done.11, pred[]{:T(512)S(6)} %eq.43), kind=kLoop, calls=%fused_computation.21 | loop fusion | flops 4194304 | bytes 16777216 | tf_op jit(solution)/shard_map/jit(_where)/select_n | solution.py:84
  295.7 6.3 %pad_maximum_fusion.4 = bf16[4,4,2,1,256,512]{5,4,1,0,3,2:T(8,128)(2,1)} fusion(bf16[4,4,1,1,256,512]{5,4,1,0,3,2:T(8,128)(2,1)} %get-tuple-element.14, bf16[4,4,1,1,256,512]{5,4,1,0,3,2:T(8,128)(2,1)S(1)} %get-tuple-element.13), kind=kLoop, calls=%fused_computation.7 | loop fusion | flops 4194304 | bytes 16777216 | tf_op jit(solution)/shard_map/concatenate | solution.py:86
  302.1 7.6 %copy.16 = bf16[4,4,2,1,256,512]{5,4,2,1,0,3:T(8,128)(2,1)} copy(bf16[4,4,2,1,256,512]{5,4,1,0,3,2:T(8,128)(2,1)} %pad_maximum_fusion.4) | data formatting | bytes 16777216 | tf_op jit(solution)/shard_map/concatenate | solution.py:86
  309.7 5.1 %select_bitcast_fusion.3 = (bf16[4,4,1,1,256,512]{5,4,2,1,0,3:T(8,128)(2,1)S(1)}, bf16[4,4,1,1,256,512]{5,4,2,1,0,3:T(8,128)(2,1)}) fusion(bf16[4,4,256,512]{3,2,1,0:T(8,128)(2,1)} %bitcast.11, bf16[4,4,256,512]{3,2,1,0:T(8,128)(2,1)} %collective-permute-done.5, pred[]{:T(512)S(6)} %eq.43), kind=kLoop, calls=%fused_computation.23 | loop fusion | flops 4194304 | bytes 16777216 | tf_op jit(solution)/shard_map/jit(_where)/select_n | solution.py:84
  314.8 6.4 %pad_maximum_fusion.3 = bf16[4,4,2,1,256,512]{5,4,2,1,0,3:T(8,128)(2,1)} fusion(bf16[4,4,1,1,256,512]{5,4,2,1,0,3:T(8,128)(2,1)} %get-tuple-element.12, bf16[4,4,1,1,256,512]{5,4,2,1,0,3:T(8,128)(2,1)S(1)} %get-tuple-element.11), kind=kLoop, calls=%fused_computation.6 | loop fusion | flops 4194304 | bytes 16777216 | tf_op jit(solution)/shard_map/concatenate | solution.py:86
  321.1 14.6 %fusion = bf16[512,8192]{0,1:T(8,128)(2,1)} fusion(bf16[512,1024]{1,0:T(8,128)(2,1)S(1)} %copy-done, bf16[8192,512]{1,0:T(8,128)(2,1)} %bitcast.157, bf16[8192,512]{1,0:T(8,128)(2,1)} %bitcast.159), kind=kOutput, calls=%fused_computation.3 | convolution fusion | flops 8627683328 | bytes 26214400 | tf_op jit(solution)/shard_map/dot_general | solution.py:104
  335.7 13.9 %fusion.8 = bf16[512,1024]{0,1:T(8,128)(2,1)S(1)} fusion(bf16[512,8192]{1,0:T(8,128)(2,1)} %param.4, bf16[8192,512]{1,0:T(8,128)(2,1)} %bitcast.158, bf16[8192,512]{1,0:T(8,128)(2,1)} %bitcast.160), kind=kOutput, calls=%fused_computation.36 | convolution fusion | flops 8624013312 | bytes 26214400 | tf_op jit(solution)/shard_map/dot_general | solution.py:103
  349.6 11.9 %copy.19 = bf16[512,8192]{1,0:T(8,128)(2,1)} copy(bf16[512,8192]{0,1:T(8,128)(2,1)} %fusion) | data formatting | bytes 16777216
  (117 shorter events, 100.2 us)
Async XLA Ops:
  33.9 94.9 %collective-permute-start.12 = (bf16[4,1024,512]{2,1,0:T(8,128)(2,1)}, bf16[4,1024,512]{2,1,0:T(8,128)(2,1)}, u32[]{:S(2)}, u32[]{:S(2)}) collective-permute-start(bf16[4,1024,512]{2,1,0:T(8,128)(2,1)} %dynamic-slice_bitcast_fusion.1), channel_id=1, source_target_pairs={{0,4},{4,0},{8,12},{12,8},{16,20},{20,16},{24,28},{28,24},{1,5},{5... | collective-permute-start | bytes 12582920 | tf_op jit(solution)/shard_map/ppermute | solution.py:40
  37.6 99.1 %collective-permute-start.18 = (bf16[4,1024,512]{2,1,0:T(8,128)(2,1)}, bf16[4,1024,512]{2,1,0:T(8,128)(2,1)}, u32[]{:S(2)}, u32[]{:S(2)}) collective-permute-start(bf16[4,1024,512]{2,1,0:T(8,128)(2,1)} %dynamic-slice_bitcast_fusion), channel_id=1, source_target_pairs={{0,4},{4,0},{8,12},{12,8},{16,20},{20,16},{24,28},{28,24},{1,5},{5... | collective-permute-start | bytes 12582920 | tf_op jit(solution)/shard_map/ppermute | solution.py:40
  46.6 12.1 %collective-permute-start.6 = (bf16[256,512]{1,0:T(8,128)(2,1)}, bf16[256,512]{1,0:T(8,128)(2,1)S(1)}, u32[]{:S(2)}, u32[]{:S(2)}) collective-permute-start(bf16[256,512]{1,0:T(8,128)(2,1)} %get-tuple-element.30), channel_id=1, source_target_pairs={{0,1},{1,2},{2,3},{3,0},{4,5},{5,6},{6,7},{7,4},{8,9},{9,10},{10,1... | collective-permute-start | bytes 786440 | tf_op jit(solution)/shard_map/ppermute | solution.py:68
  49.1 20.7 %collective-permute-start.7 = (bf16[256,512]{1,0:T(8,128)(2,1)}, bf16[256,512]{1,0:T(8,128)(2,1)S(1)}, u32[]{:S(2)}, u32[]{:S(2)}) collective-permute-start(bf16[256,512]{1,0:T(8,128)(2,1)} %get-tuple-element.30), channel_id=1, source_target_pairs={{0,2},{1,3},{2,0},{3,1},{4,6},{5,7},{6,4},{7,5},{8,10},{9,11},{10,... | collective-permute-start | bytes 786440 | tf_op jit(solution)/shard_map/ppermute | solution.py:68
  51.7 19.1 %collective-permute-start.8 = (bf16[256,512]{1,0:T(8,128)(2,1)}, bf16[256,512]{1,0:T(8,128)(2,1)S(1)}, u32[]{:S(2)}, u32[]{:S(2)}) collective-permute-start(bf16[256,512]{1,0:T(8,128)(2,1)} %get-tuple-element.30), channel_id=1, source_target_pairs={{0,3},{1,0},{2,1},{3,2},{4,7},{5,4},{6,5},{7,6},{8,11},{9,8},{10,9... | collective-permute-start | bytes 786440 | tf_op jit(solution)/shard_map/ppermute | solution.py:68
  58.7 24.5 %collective-permute-start = (bf16[256,512]{1,0:T(8,128)(2,1)}, bf16[256,512]{1,0:T(8,128)(2,1)S(1)}, u32[]{:S(2)}, u32[]{:S(2)}) collective-permute-start(bf16[256,512]{1,0:T(8,128)(2,1)} %get-tuple-element.29), channel_id=1, source_target_pairs={{0,1},{1,2},{2,3},{3,0},{4,5},{5,6},{6,7},{7,4},{8,9},{9,10},{10,1... | collective-permute-start | bytes 786440 | tf_op jit(solution)/shard_map/ppermute | solution.py:68
  69.9 22.3 %collective-permute-start.1 = (bf16[256,512]{1,0:T(8,128)(2,1)}, bf16[256,512]{1,0:T(8,128)(2,1)S(1)}, u32[]{:S(2)}, u32[]{:S(2)}) collective-permute-start(bf16[256,512]{1,0:T(8,128)(2,1)} %get-tuple-element.29), channel_id=1, source_target_pairs={{0,2},{1,3},{2,0},{3,1},{4,6},{5,7},{6,4},{7,5},{8,10},{9,11},{10,... | collective-permute-start | bytes 786440 | tf_op jit(solution)/shard_map/ppermute | solution.py:68
  70.8 24.7 %collective-permute-start.2 = (bf16[256,512]{1,0:T(8,128)(2,1)}, bf16[256,512]{1,0:T(8,128)(2,1)S(1)}, u32[]{:S(2)}, u32[]{:S(2)}) collective-permute-start(bf16[256,512]{1,0:T(8,128)(2,1)} %get-tuple-element.29), channel_id=1, source_target_pairs={{0,3},{1,0},{2,1},{3,2},{4,7},{5,4},{6,5},{7,6},{8,11},{9,8},{10,9... | collective-permute-start | bytes 786440 | tf_op jit(solution)/shard_map/ppermute | solution.py:68
  83.2 20.6 %collective-permute-start.9 = (bf16[4,1,256,512]{3,2,0,1:T(8,128)(2,1)S(1)}, bf16[4,1,256,512]{3,2,0,1:T(8,128)(2,1)}, u32[]{:S(2)}, u32[]{:S(2)}) collective-permute-start(bf16[4,1,256,512]{3,2,0,1:T(8,128)(2,1)S(1)} %bitcast.161), channel_id=1, source_target_pairs={{0,16},{4,20},{8,24},{12,28},{16,0},{20,4},{24,8},{28,12},{1,17},{... | collective-permute-start | bytes 3145736 | tf_op jit(solution)/shard_map/ppermute | solution.py:79
  96.3 26.4 %collective-permute-start.3 = (bf16[4,1,256,512]{3,2,0,1:T(8,128)(2,1)}, bf16[4,1,256,512]{3,2,0,1:T(8,128)(2,1)}, u32[]{:S(2)}, u32[]{:S(2)}) collective-permute-start(bf16[4,1,256,512]{3,2,0,1:T(8,128)(2,1)} %bitcast.162), channel_id=1, source_target_pairs={{0,8},{4,12},{8,0},{12,4},{16,24},{20,28},{24,16},{28,20},{1,9},{5... | collective-permute-start | bytes 3145736 | tf_op jit(solution)/shard_map/ppermute | solution.py:79
  106.9 60.7 %collective-permute-start.10 = (bf16[4,2,256,512]{3,2,1,0:T(8,128)(2,1)}, bf16[4,2,256,512]{3,2,1,0:T(8,128)(2,1)}, u32[]{:S(2)}, u32[]{:S(2)}) collective-permute-start(bf16[4,2,256,512]{3,2,1,0:T(8,128)(2,1)} %maximum_bitcast_fusion.1), channel_id=1, source_target_pairs={{0,8},{4,12},{8,0},{12,4},{16,24},{20,28},{24,16},{28,20},{1,9},{5... | collective-permute-start | bytes 6291464 | tf_op jit(solution)/shard_map/ppermute | solution.py:79
  127.2 48.9 %collective-permute-start.4 = (bf16[4,2,256,512]{3,2,0,1:T(8,128)(2,1)}, bf16[4,2,256,512]{3,2,0,1:T(8,128)(2,1)}, u32[]{:S(2)}, u32[]{:S(2)}) collective-permute-start(bf16[4,2,256,512]{3,2,0,1:T(8,128)(2,1)} %maximum_bitcast_fusion), channel_id=1, source_target_pairs={{0,16},{4,20},{8,24},{12,28},{16,0},{20,4},{24,8},{28,12},{1,17},{... | collective-permute-start | bytes 6291464 | tf_op jit(solution)/shard_map/ppermute | solution.py:79
  135.2 76.0 %collective-permute-start.13 = (bf16[2,1024,512]{2,1,0:T(8,128)(2,1)}, bf16[2,1024,512]{2,1,0:T(8,128)(2,1)}, u32[]{:S(2)}, u32[]{:S(2)}) collective-permute-start(bf16[2,1024,512]{2,1,0:T(8,128)(2,1)} %dynamic-slice_bitcast_fusion.3), channel_id=1, source_target_pairs={{0,8},{4,12},{8,0},{12,4},{16,24},{20,28},{24,16},{28,20},{1,9},{5... | collective-permute-start | bytes 6291464 | tf_op jit(solution)/shard_map/ppermute | solution.py:40
  141.9 76.9 %collective-permute-start.19 = (bf16[1,2048,512]{2,1,0:T(8,128)(2,1)}, bf16[1,2048,512]{2,1,0:T(8,128)(2,1)}, u32[]{:S(2)}, u32[]{:S(2)}) collective-permute-start(bf16[1,2048,512]{2,1,0:T(8,128)(2,1)} %dynamic-slice_bitcast_fusion.2), channel_id=1, source_target_pairs={{0,16},{4,20},{8,24},{12,28},{16,0},{20,4},{24,8},{28,12},{1,17},{... | collective-permute-start | bytes 6291464 | tf_op jit(solution)/shard_map/ppermute | solution.py:40
  171.9 118.7 %collective-permute-start.11 = (bf16[4,4,256,512]{3,2,1,0:T(8,128)(2,1)}, bf16[4,4,256,512]{3,2,1,0:T(8,128)(2,1)}, u32[]{:S(2)}, u32[]{:S(2)}) collective-permute-start(bf16[4,4,256,512]{3,2,1,0:T(8,128)(2,1)} %bitcast.29), channel_id=1, source_target_pairs={{0,4},{4,0},{8,12},{12,8},{16,20},{20,16},{24,28},{28,24},{1,5},{5... | collective-permute-start | bytes 12582920 | tf_op jit(solution)/shard_map/ppermute | solution.py:79
  181.0 128.7 %collective-permute-start.5 = (bf16[4,4,256,512]{3,2,1,0:T(8,128)(2,1)}, bf16[4,4,256,512]{3,2,1,0:T(8,128)(2,1)}, u32[]{:S(2)}, u32[]{:S(2)}) collective-permute-start(bf16[4,4,256,512]{3,2,1,0:T(8,128)(2,1)} %bitcast.11), channel_id=1, source_target_pairs={{0,4},{4,0},{8,12},{12,8},{16,20},{20,16},{24,28},{28,24},{1,5},{5... | collective-permute-start | bytes 12582920 | tf_op jit(solution)/shard_map/ppermute | solution.py:79
  214.6 25.4 %collective-permute-start.14 = (bf16[1,1024,512]{2,1,0:T(8,128)(2,1)}, bf16[1,1024,512]{2,1,0:T(8,128)(2,1)}, u32[]{:S(2)}, u32[]{:S(2)}) collective-permute-start(bf16[1,1024,512]{2,1,0:T(8,128)(2,1)} %constant_dynamic-slice_fusion), channel_id=1, source_target_pairs={{0,16},{4,20},{8,24},{12,28},{16,0},{20,4},{24,8},{28,12},{1,17},{... | collective-permute-start | bytes 3145736 | tf_op jit(solution)/shard_map/ppermute | solution.py:40
  222.0 25.1 %collective-permute-start.20 = (bf16[1,1024,512]{2,1,0:T(8,128)(2,1)}, bf16[1,1024,512]{2,1,0:T(8,128)(2,1)}, u32[]{:S(2)}, u32[]{:S(2)}) collective-permute-start(bf16[1,1024,512]{2,1,0:T(8,128)(2,1)} %dynamic-slice_bitcast_fusion.4), channel_id=1, source_target_pairs={{0,8},{4,12},{8,0},{12,4},{16,24},{20,28},{24,16},{28,20},{1,9},{5... | collective-permute-start | bytes 3145736 | tf_op jit(solution)/shard_map/ppermute | solution.py:40
  242.0 11.9 %collective-permute-start.15 = (bf16[256,512]{1,0:T(8,128)(2,1)S(1)}, bf16[256,512]{1,0:T(8,128)(2,1)S(1)}, u32[]{:S(2)}, u32[]{:S(2)}) collective-permute-start(bf16[256,512]{1,0:T(8,128)(2,1)S(1)} %get-tuple-element.23), channel_id=1, source_target_pairs={{0,1},{1,2},{2,3},{3,0},{4,5},{5,6},{6,7},{7,4},{8,9},{9,10},{10,1... | collective-permute-start | bytes 786440 | tf_op jit(solution)/shard_map/ppermute | solution.py:49
  245.7 19.4 %collective-permute-start.16 = (bf16[256,512]{1,0:T(8,128)(2,1)S(1)}, bf16[256,512]{1,0:T(8,128)(2,1)S(1)}, u32[]{:S(2)}, u32[]{:S(2)}) collective-permute-start(bf16[256,512]{1,0:T(8,128)(2,1)S(1)} %get-tuple-element.25), channel_id=1, source_target_pairs={{0,2},{1,3},{2,0},{3,1},{4,6},{5,7},{6,4},{7,5},{8,10},{9,11},{10,... | collective-permute-start | bytes 786440 | tf_op jit(solution)/shard_map/ppermute | solution.py:49
  247.1 18.0 %collective-permute-start.17 = (bf16[256,512]{1,0:T(8,128)(2,1)S(1)}, bf16[256,512]{1,0:T(8,128)(2,1)S(1)}, u32[]{:S(2)}, u32[]{:S(2)}) collective-permute-start(bf16[256,512]{1,0:T(8,128)(2,1)S(1)} %get-tuple-element.24), channel_id=1, source_target_pairs={{0,3},{1,0},{2,1},{3,2},{4,7},{5,4},{6,5},{7,6},{8,11},{9,8},{10,9... | collective-permute-start | bytes 786440 | tf_op jit(solution)/shard_map/ppermute | solution.py:49
  253.9 29.3 %collective-permute-start.21 = (bf16[256,512]{1,0:T(8,128)(2,1)S(1)}, bf16[256,512]{1,0:T(8,128)(2,1)S(1)}, u32[]{:S(2)}, u32[]{:S(2)}) collective-permute-start(bf16[256,512]{1,0:T(8,128)(2,1)S(1)} %get-tuple-element.26), channel_id=1, source_target_pairs={{0,1},{1,2},{2,3},{3,0},{4,5},{5,6},{6,7},{7,4},{8,9},{9,10},{10,1... | collective-permute-start | bytes 786440 | tf_op jit(solution)/shard_map/ppermute | solution.py:49
  265.1 20.7 %collective-permute-start.22 = (bf16[256,512]{1,0:T(8,128)(2,1)S(1)}, bf16[256,512]{1,0:T(8,128)(2,1)S(1)}, u32[]{:S(2)}, u32[]{:S(2)}) collective-permute-start(bf16[256,512]{1,0:T(8,128)(2,1)S(1)} %get-tuple-element.28), channel_id=1, source_target_pairs={{0,2},{1,3},{2,0},{3,1},{4,6},{5,7},{6,4},{7,5},{8,10},{9,11},{10,... | collective-permute-start | bytes 786440 | tf_op jit(solution)/shard_map/ppermute | solution.py:49
  266.5 22.0 %collective-permute-start.23 = (bf16[256,512]{1,0:T(8,128)(2,1)S(1)}, bf16[256,512]{1,0:T(8,128)(2,1)S(1)}, u32[]{:S(2)}, u32[]{:S(2)}) collective-permute-start(bf16[256,512]{1,0:T(8,128)(2,1)S(1)} %get-tuple-element.27), channel_id=1, source_target_pairs={{0,3},{1,0},{2,1},{3,2},{4,7},{5,4},{6,5},{7,6},{8,11},{9,8},{10,9... | collective-permute-start | bytes 786440 | tf_op jit(solution)/shard_map/ppermute | solution.py:49
  (20 other events, 182.7 us)

commit v2 on v0

v2 whole, which is shorter than its diff:
```python
import jax
import jax.numpy as jnp
from jax import lax
from jax.sharding import Mesh, PartitionSpec as P

CHUNKS = 2


def dequantized(weight_codes, block_scales):
    row_count, col_count = weight_codes.shape
    row_blocks, col_blocks = block_scales.shape
    scaled = (
        weight_codes.astype(jnp.float32).reshape(
            row_blocks, row_count // row_blocks, col_blocks, col_count // col_blocks
        )
        * block_scales[:, None, :, None]
    )
    return scaled.reshape(row_count, col_count).astype(jnp.bfloat16)


def halved(view, mine, axis_name, pairs):
    going = lax.dynamic_index_in_dim(view, 1 - mine, 1, keepdims=False)
    kept = lax.dynamic_index_in_dim(view, mine, 1, keepdims=False)
    came = lax.ppermute(going, axis_name, pairs)
    return (kept.astype(jnp.float32) + came.astype(jnp.float32)).astype(jnp.bfloat16)


def dp_sum(block, turn):
    chip_index = lax.axis_index("chip")
    chip_count = lax.axis_size("chip")
    width = block.shape[1]
    inner = block.shape[0] // (chip_count * 2)
    block = halved(block.reshape(chip_count, 2, inner, width), lax.axis_index("core"), "core", [(0, 1), (1, 0)])
    left = list(range(chip_count.bit_length() - 1))
    turn = turn % len(left) if left else 0
    for bit in left[turn:] + left[:turn]:
        stride = 1 << bit
        pairs = [(i, i ^ stride) for i in range(chip_count)]
        lower = inner << sum(1 for other in left if other < bit)
        block = halved(block.reshape(-1, 2, lower, width), (chip_index // stride) % 2, "chip", pairs)
        left = [other for other in left if other != bit]
    return block.reshape(inner, width)


def node_sum(block):
    node_index = lax.axis_index("node")
    node_count = lax.axis_size("node")
    view = block.reshape(node_count, -1, block.shape[1])
    total = lax.dynamic_index_in_dim(view, node_index, 0, keepdims=False).astype(jnp.float32)
    for shift in range(1, node_count):
        going = lax.dynamic_index_in_dim(view, (node_index + shift) % node_count, 0, keepdims=False)
        pairs = [(i, (i + shift) % node_count) for i in range(node_count)]
        total = total + lax.ppermute(going, "node", pairs).astype(jnp.float32)
    return total


def shards(tokens, weight_codes, block_scales, value_grad):
    chip_count = lax.axis_size("chip")
    core_index = lax.axis_index("core")
    total_tokens = tokens.shape[0] * chip_count * 2 * lax.axis_size("node")
    local_weight = dequantized(weight_codes, block_scales)
    part = local_weight.shape[0] // (chip_count * 2)
    place = lax.axis_index("chip") * 2 + core_index
    piece = lax.dynamic_slice_in_dim(local_weight, place * part, part, 0)
    tokens, value_grad, piece = lax.optimization_barrier((tokens, value_grad, piece))
    full_weight = lax.all_gather(piece, ("node", "chip", "core"), axis=0, tiled=True)
    width = value_grad.shape[1] // CHUNKS
    blocks = []
    for chunk in range(CHUNKS):
        product = lax.dot_general(
            tokens,
            value_grad[:, chunk * width:(chunk + 1) * width],
            (((0,), (0,)), ((), ())),
            preferred_element_type=jnp.float32,
        )
        blocks.append(dp_sum((product * total_tokens ** (-0.5)).astype(jnp.bfloat16), chunk))
    full_weight, *blocks = lax.optimization_barrier((full_weight, *blocks))
    input_grad = lax.dot_general(
        value_grad, full_weight, (((1,), (1,)), ((), ())), preferred_element_type=jnp.float32
    ).astype(jnp.bfloat16)
    input_grad, blocks[-1] = lax.optimization_barrier((input_grad, blocks[-1]))
    values = jnp.dot(tokens, full_weight, preferred_element_type=jnp.float32).astype(jnp.bfloat16)
    weight_grad = jnp.concatenate([node_sum(block) for block in blocks], axis=1)
    return (values, input_grad, weight_grad)


def solution(mesh):
    dp, node = mesh.devices.shape
    cores = Mesh(mesh.devices.reshape(dp // 2, 2, node), ("chip", "core", "node"))
    rows = P(("chip", "core", "node"), None)
    in_specs = (rows, P("node", None), P("node", None), rows)
    return jax.shard_map(shards, mesh=cores, in_specs=in_specs, out_specs=(rows, rows, rows), check_vma=False)
```

time: 564 us -> 222 us (0.39)
  blocking collectives: 245 us -> 0 us
  other arithmetic: 127 us -> 21.4 us
  local copies, waits for them, and re-layouts: 125 us -> 24.2 us
  waiting for transfers between devices: 0.02 us -> 96.3 us
  starting transfers between devices: 0.04 us -> 16 us
    all_to_all x2 -> x0, blocking collectives: 245 us -> none  [the longest x1 192 us: shards(): lax.all_to_all(grad_term[None], 'dp', split_axis=1, concat_axis=0, tiled=...]
    unnamed x2 -> x0, other arithmetic: 109 us -> none
    ppermute x0 -> x12, waiting for transfers between devices: none -> 96.3 us  [the longest x6 91.4 us: halved(): came = lax.ppermute(going, axis_name, pairs)]
    unnamed x14 -> x16, local copies, waits for them, and re-layouts: 89.7 us -> 15.8 us
    broadcast_in_dim x1 -> x0, local copies, waits for them, and re-layouts: 29.2 us -> none  [shards(): grad_term[None]]
    ppermute x0 -> x12, starting transfers between devices: none -> 16 us  [the longest x6 8.26 us: node_sum(): total = total + lax.ppermute(going, 'node', pairs).astype(jnp.float32)]
    reduce_sum x2 -> x0, other arithmetic: 13.1 us -> none  [the longest x1 9.46 us: shards(): partial_value = jnp.sum(first_hop, axis=0, dtype=jnp.float32)]
    convert_element_type x1 -> x5, other arithmetic: 4.19 us -> 16.7 us  [the longest x4 14.4 us: halved(): (kept.astype(jnp.float32) + came.astype(jnp.float32)).astype(jnp.bfloat16)]
  transfers between devices with their start and end apart: 1 -> 13, of which waited for: 0 -> 5; matrix products, arithmetic and copies ran while one was open for 44% -> 33% of each run, Pallas kernels for 0% -> 0%
where the time goes in v2:
time: 222 us; the launch traced here: 219 us
  waiting for transfers between devices  96.3 us (43%)
  matrix products  47 us (21%)
  local copies, waits for them, and re-layouts  24.2 us (11%)
  other arithmetic  21.4 us (10%)
  starting transfers between devices  16 us (7%)
  between operations  14.2 us (6%)
    ppermute x6, waiting for transfers between devices, halved(): came = lax.ppermute(going, axis_name, pairs)  91.4 us
    dot_general x2, matrix products, shards(): lax.dot_general(tokens, value_grad[:, chunk * width:(chunk + 1) * width],...  16.7 us
    unnamed x16, local copies, waits for them, and re-layouts  15.8 us
    dot_general x1, matrix products, shards(): jnp.dot(tokens, full_weight, preferred_element_type=jnp.float32)  15.6 us
    dot_general x1, matrix products, shards(): lax.dot_general(value_grad, full_weight, (((1,), (1,)), ((), ())), prefer...  14.7 us
    convert_element_type x4, other arithmetic, halved(): (kept.astype(jnp.float32) + came.astype(jnp.float32)).astype(jnp.bfloat16)  14.4 us
    ppermute x6, starting transfers between devices, node_sum(): total = total + lax.ppermute(going, 'node', pairs).astype(jnp.float32)  8.26 us
    ppermute x6, starting transfers between devices, halved(): came = lax.ppermute(going, axis_name, pairs)  7.72 us
  transfers between devices with their start and end apart: 13, of which 5 were waited for; matrix products, arithmetic and copies ran while one was open for 33% of the time, Pallas kernels for 0%

profile of v2, /device:TPU:0, one launch (start us, length us, event | category | flops | bytes accessed | tf_op | source)
XLA Modules:
  0.0 219.1 jit_solution(13400799029170271523)
XLA Ops:
  8.6 5.5 %copy.12 = f32[256,8,8,128]{3,1,2,0:T(8,128)} copy(f32[256,8,8,128]{3,2,1,0:T(8,128)S(1)} %bitcast.67) | data formatting | bytes 16777216
  14.1 2.3 %fusion.7 = bf16[256,1024]{1,0:T(8,128)(2,1)} fusion(f32[2048,1024]{1,0:T(8,128)} %bitcast.72, s32[]{:T(128)S(6)} %select_n.88, bf16[2048,1024]{1,0:T(8,128)(2,1)} %param.5), kind=kLoop, calls=%fused_computation.23 | loop fusion | flops 786432 | bytes 2097156 | tf_op jit(solution)/shard_map/convert_element_type | solution.py:18
  16.4 8.5 %multiply_convert_fusion = bf16[8192,512]{1,0:T(8,128)(2,1)S(1)} fusion(bf16[512,8192]{1,0:T(8,128)(2,1)} %param.4, bf16[512,1024]{1,0:T(8,128)(2,1)S(1)} %copy-done.6), kind=kOutput, calls=%fused_computation | convolution fusion | flops 4303355904 | bytes 17301504 | tf_op jit(solution)/shard_map/dot_general | solution.py:70
  24.9 2.5 %dynamic-slice_bitcast_fusion = bf16[4,1024,512]{2,1,0:T(8,128)(2,1)} fusion(bf16[4,2,1024,512]{3,2,1,0:T(8,128)(2,1)S(1)} %bitcast.77, s32[]{:T(128)S(6)} %select_n.90), kind=kLoop, calls=%fused_computation.12 | loop fusion | bytes 8388612 | tf_op jit(solution)/shard_map/jit(dynamic_index_in_dim)/squeeze | solution.py:22
  27.4 2.2 %copy-done.5 = bf16[8192,512]{1,0:T(8,128)(2,1)} copy-done((bf16[8192,512]{1,0:T(8,128)(2,1)}, bf16[8192,512]{1,0:T(8,128)(2,1)S(1)}, u32[]{:S(2)}) %copy-start.5) | copy-done | bytes 8388632
  30.0 8.2 %multiply_convert_fusion.1 = bf16[8192,512]{1,0:T(8,128)(2,1)S(1)} fusion(bf16[512,8192]{1,0:T(8,128)(2,1)} %param.4, bf16[512,1024]{1,0:T(8,128)(2,1)S(1)} %copy-done.6), kind=kOutput, calls=%fused_computation.1 | convolution fusion | flops 4303355904 | bytes 17301504 | tf_op jit(solution)/shard_map/dot_general | solution.py:70
  38.3 2.5 %dynamic-slice_bitcast_fusion.1 = bf16[4,1024,512]{2,1,0:T(8,128)(2,1)} fusion(bf16[4,2,1024,512]{3,2,1,0:T(8,128)(2,1)S(1)} %bitcast.75, s32[]{:T(128)S(6)} %select_n.90), kind=kLoop, calls=%fused_computation.13 | loop fusion | bytes 8388612 | tf_op jit(solution)/shard_map/jit(dynamic_index_in_dim)/squeeze | solution.py:22
  40.7 2.0 copy-done.4
  42.9 4.7 %fusion = bf16[4,1024,512]{2,1,0:T(8,128)(2,1)S(1)} fusion(bf16[4,1024,512]{2,1,0:T(8,128)(2,1)} %collective-permute-done.3, bf16[4,2,1024,512]{3,2,1,0:T(8,128)(2,1)} %bitcast.78, s32[]{:T(128)S(6)} %select_n.89), kind=kLoop, calls=%fused_computation.5 | loop fusion | flops 8388608 | bytes 12582916 | tf_op jit(solution)/shard_map/convert_element_type | solution.py:25
  47.6 2.0 copy-done
  49.7 3.1 %collective-permute-start.4 = (bf16[1,2048,512]{2,1,0:T(8,128)(2,1)S(1)}, bf16[1,2048,512]{2,1,0:T(8,128)(2,1)}, u32[]{:S(2)}, u32[]{:S(2)}) collective-permute-start(bf16[1,2048,512]{2,1,0:T(8,128)(2,1)S(1)} %dynamic-slice_bitcast_fusion.2), channel_id=1, source_target_pairs={{0,16},{8,24},{16,0},{24,8},{1,17},{9,25},{17,1},{25,9},{2,18},{10... | collective-permute-start | bytes 6291464 | tf_op jit(solution)/shard_map/ppermute | solution.py:24
  52.8 4.7 %fusion.1 = bf16[4,1024,512]{2,1,0:T(8,128)(2,1)S(1)} fusion(bf16[4,1024,512]{2,1,0:T(8,128)(2,1)} %collective-permute-done, bf16[4,2,1024,512]{3,2,1,0:T(8,128)(2,1)} %bitcast.76, s32[]{:T(128)S(6)} %select_n.89), kind=kLoop, calls=%fused_computation.7 | loop fusion | flops 8388608 | bytes 12582916 | tf_op jit(solution)/shard_map/convert_element_type | solution.py:25
  57.5 1.9 copy-done.1
  62.4 58.9 %collective-permute-done.4 = bf16[1,2048,512]{2,1,0:T(8,128)(2,1)} collective-permute-done((bf16[1,2048,512]{2,1,0:T(8,128)(2,1)S(1)}, bf16[1,2048,512]{2,1,0:T(8,128)(2,1)}, u32[]{:S(2)}, u32[]{:S(2)}) %collective-permute-start.4) | collective-permute-done | bytes 2097184 | tf_op jit(solution)/shard_map/ppermute | solution.py:24
  121.4 2.8 %fusion.2 = bf16[1,2048,512]{2,1,0:T(8,128)(2,1)S(1)} fusion(bf16[1,2048,512]{2,1,0:T(8,128)(2,1)} %collective-permute-done.4, bf16[1,2,2048,512]{3,2,1,0:T(8,128)(2,1)} %bitcast.69, s32[]{:T(128)S(6)} %select_n.96), kind=kLoop, calls=%fused_computation.9 | loop fusion | flops 4194304 | bytes 6291460 | tf_op jit(solution)/shard_map/convert_element_type | solution.py:25
  125.9 11.0 %collective-permute-done.1 = bf16[2,1024,512]{2,1,0:T(8,128)(2,1)} collective-permute-done((bf16[2,1024,512]{2,1,0:T(8,128)(2,1)}, bf16[2,1024,512]{2,1,0:T(8,128)(2,1)}, u32[]{:S(2)}, u32[]{:S(2)}) %collective-permute-start.1) | collective-permute-done | bytes 2097184 | tf_op jit(solution)/shard_map/ppermute | solution.py:24
  136.9 2.2 fusion.3
  142.5 20.6 %collective-permute-done.5 = bf16[1,1024,512]{2,1,0:T(8,128)(2,1)} collective-permute-done((bf16[1,1024,512]{2,1,0:T(8,128)(2,1)S(1)}, bf16[1,1024,512]{2,1,0:T(8,128)(2,1)}, u32[]{:S(2)}, u32[]{:S(2)}) %collective-permute-start.5) | collective-permute-done | bytes 1048608 | tf_op jit(solution)/shard_map/ppermute | solution.py:24
  165.4 1.8 fusion.5
  168.8 2.4 %collective-permute-start.7 = (bf16[256,512]{1,0:T(8,128)(2,1)S(1)}, bf16[256,512]{1,0:T(8,128)(2,1)S(1)}, u32[]{:S(2)}, u32[]{:S(2)}) collective-permute-start(bf16[256,512]{1,0:T(8,128)(2,1)S(1)} %get-tuple-element.21), channel_id=1, source_target_pairs={{0,2},{1,3},{2,0},{3,1},{4,6},{5,7},{6,4},{7,5},{8,10},{9,11},{10,... | collective-permute-start | bytes 786440 | tf_op jit(solution)/shard_map/ppermute | solution.py:53
  172.6 14.7 %convolution_convert_fusion = bf16[512,8192]{1,0:T(8,128)(2,1)} fusion(bf16[512,1024]{1,0:T(8,128)(2,1)} %param.7, bf16[8192,1024]{1,0:T(8,128)(2,1)} %all-gather.2.cloned.1.call-done), kind=kOutput, calls=%fused_computation.2 | convolution fusion | flops 8594128896 | bytes 26214400 | tf_op jit(solution)/shard_map/dot_general | solution.py:78
  188.1 2.3 %collective-permute-start.11 = (bf16[256,512]{1,0:T(8,128)(2,1)S(1)}, bf16[256,512]{1,0:T(8,128)(2,1)S(1)}, u32[]{:S(2)}, u32[]{:S(2)}) collective-permute-start(bf16[256,512]{1,0:T(8,128)(2,1)S(1)} %get-tuple-element.23), channel_id=1, source_target_pairs={{0,3},{1,0},{2,1},{3,2},{4,7},{5,4},{6,5},{7,6},{8,11},{9,8},{10,9... | collective-permute-start | bytes 786440 | tf_op jit(solution)/shard_map/ppermute | solution.py:53
  190.4 15.6 %convolution_convert_fusion.1 = bf16[512,1024]{1,0:T(8,128)(2,1)} fusion(bf16[512,8192]{1,0:T(8,128)(2,1)} %param.4, bf16[8192,1024]{1,0:T(8,128)(2,1)} %all-gather.2.cloned.1.call-done), kind=kOutput, calls=%fused_computation.19 | convolution fusion | flops 8590458880 | bytes 26214400 | tf_op jit(solution)/shard_map/dot_general | solution.py:82
  206.1 4.9 %collective-permute-done.10 = bf16[256,512]{1,0:T(8,128)(2,1)S(1)} collective-permute-done((bf16[256,512]{1,0:T(8,128)(2,1)S(1)}, bf16[256,512]{1,0:T(8,128)(2,1)S(1)}, u32[]{:S(2)}, u32[]{:S(2)}) %collective-permute-start.10) | collective-permute-done | bytes 262176 | tf_op jit(solution)/shard_map/ppermute | solution.py:53
  (42 shorter events, 17.6 us)
Async XLA Ops:
  7.2 160.1 %all-gather.2.cloned.1.call-start = ((), (), s32[]{:S(2)}) async-start(), calls=%async_computation | async-start | bytes 17301504 | tf_op jit(solution)/shard_map/all_gather | solution.py:66
  8.6 7.8 %copy-start.6 = (bf16[512,1024]{1,0:T(8,128)(2,1)S(1)}, bf16[512,1024]{1,0:T(8,128)(2,1)}, u32[]{:S(2)}) copy-start(bf16[512,1024]{1,0:T(8,128)(2,1)} %param.7) | copy-start | bytes 3145732
  24.9 4.7 %copy-start.5 = (bf16[8192,512]{1,0:T(8,128)(2,1)}, bf16[8192,512]{1,0:T(8,128)(2,1)S(1)}, u32[]{:S(2)}) copy-start(bf16[8192,512]{1,0:T(8,128)(2,1)S(1)} %multiply_convert_fusion) | copy-start | bytes 25165828
  29.6 13.3 %collective-permute-start.3 = (bf16[4,1024,512]{2,1,0:T(8,128)(2,1)}, bf16[4,1024,512]{2,1,0:T(8,128)(2,1)}, u32[]{:S(2)}, u32[]{:S(2)}) collective-permute-start(bf16[4,1024,512]{2,1,0:T(8,128)(2,1)} %dynamic-slice_bitcast_fusion), channel_id=1, source_target_pairs={{0,4},{4,0},{1,5},{5,1},{2,6},{6,2},{3,7},{7,3},{8,12},{12,8},{9,1... | collective-permute-start | bytes 12582920 | tf_op jit(solution)/shard_map/ppermute | solution.py:24
  38.3 4.5 %copy-start.4 = (bf16[8192,512]{1,0:T(8,128)(2,1)}, bf16[8192,512]{1,0:T(8,128)(2,1)S(1)}, u32[]{:S(2)}) copy-start(bf16[8192,512]{1,0:T(8,128)(2,1)S(1)} %multiply_convert_fusion.1) | copy-start | bytes 25165828
  42.8 10.0 %collective-permute-start = (bf16[4,1024,512]{2,1,0:T(8,128)(2,1)}, bf16[4,1024,512]{2,1,0:T(8,128)(2,1)}, u32[]{:S(2)}, u32[]{:S(2)}) collective-permute-start(bf16[4,1024,512]{2,1,0:T(8,128)(2,1)} %dynamic-slice_bitcast_fusion.1), channel_id=1, source_target_pairs={{0,4},{4,0},{1,5},{5,1},{2,6},{6,2},{3,7},{7,3},{8,12},{12,8},{9,1... | collective-permute-start | bytes 12582920 | tf_op jit(solution)/shard_map/ppermute | solution.py:24
  47.5 2.0 copy-start
  49.7 71.7 %collective-permute-start.4 = (bf16[1,2048,512]{2,1,0:T(8,128)(2,1)S(1)}, bf16[1,2048,512]{2,1,0:T(8,128)(2,1)}, u32[]{:S(2)}, u32[]{:S(2)}) collective-permute-start(bf16[1,2048,512]{2,1,0:T(8,128)(2,1)S(1)} %dynamic-slice_bitcast_fusion.2), channel_id=1, source_target_pairs={{0,16},{8,24},{16,0},{24,8},{1,17},{9,25},{17,1},{25,9},{2,18},{10... | collective-permute-start | bytes 6291464 | tf_op jit(solution)/shard_map/ppermute | solution.py:24
  57.5 1.9 copy-start.1
  61.0 75.9 %collective-permute-start.1 = (bf16[2,1024,512]{2,1,0:T(8,128)(2,1)}, bf16[2,1024,512]{2,1,0:T(8,128)(2,1)}, u32[]{:S(2)}, u32[]{:S(2)}) collective-permute-start(bf16[2,1024,512]{2,1,0:T(8,128)(2,1)} %dynamic-slice_bitcast_fusion.3), channel_id=1, source_target_pairs={{0,8},{8,0},{16,24},{24,16},{1,9},{9,1},{17,25},{25,17},{2,10},{10... | collective-permute-start | bytes 6291464 | tf_op jit(solution)/shard_map/ppermute | solution.py:24
  62.4 74.5 %copy-start.2 = (bf16[4,1024,512]{2,1,0:T(8,128)(2,1)S(1)}, bf16[4,1024,512]{2,1,0:T(8,128)(2,1)}, u32[]{:S(2)}) copy-start(bf16[4,1024,512]{2,1,0:T(8,128)(2,1)} %copy-done.1) | copy-start | bytes 12582916
  124.3 38.8 %collective-permute-start.5 = (bf16[1,1024,512]{2,1,0:T(8,128)(2,1)S(1)}, bf16[1,1024,512]{2,1,0:T(8,128)(2,1)}, u32[]{:S(2)}, u32[]{:S(2)}) collective-permute-start(bf16[1,1024,512]{2,1,0:T(8,128)(2,1)S(1)} %dynamic-slice_bitcast_fusion.4), channel_id=1, source_target_pairs={{0,8},{8,0},{16,24},{24,16},{1,9},{9,1},{17,25},{25,17},{2,10},{10... | collective-permute-start | bytes 3145736 | tf_op jit(solution)/shard_map/ppermute | solution.py:24
  139.1 1.3 copy-start.3
  141.4 24.0 %collective-permute-start.2 = (bf16[1,1024,512]{2,1,0:T(8,128)(2,1)}, bf16[1,1024,512]{2,1,0:T(8,128)(2,1)}, u32[]{:S(2)}, u32[]{:S(2)}) collective-permute-start(bf16[1,1024,512]{2,1,0:T(8,128)(2,1)} %constant_dynamic-slice_fusion), channel_id=1, source_target_pairs={{0,16},{8,24},{16,0},{24,8},{1,17},{9,25},{17,1},{25,9},{2,18},{10... | collective-permute-start | bytes 3145736 | tf_op jit(solution)/shard_map/ppermute | solution.py:24
  167.4 23.0 %collective-permute-start.6 = (bf16[256,512]{1,0:T(8,128)(2,1)S(1)}, bf16[256,512]{1,0:T(8,128)(2,1)S(1)}, u32[]{:S(2)}, u32[]{:S(2)}) collective-permute-start(bf16[256,512]{1,0:T(8,128)(2,1)S(1)} %get-tuple-element.19), channel_id=1, source_target_pairs={{0,1},{1,2},{2,3},{3,0},{4,5},{5,6},{6,7},{7,4},{8,9},{9,10},{10,1... | collective-permute-start | bytes 786440 | tf_op jit(solution)/shard_map/ppermute | solution.py:53
  168.8 37.2 %collective-permute-start.7 = (bf16[256,512]{1,0:T(8,128)(2,1)S(1)}, bf16[256,512]{1,0:T(8,128)(2,1)S(1)}, u32[]{:S(2)}, u32[]{:S(2)}) collective-permute-start(bf16[256,512]{1,0:T(8,128)(2,1)S(1)} %get-tuple-element.21), channel_id=1, source_target_pairs={{0,2},{1,3},{2,0},{3,1},{4,6},{5,7},{6,4},{7,5},{8,10},{9,11},{10,... | collective-permute-start | bytes 786440 | tf_op jit(solution)/shard_map/ppermute | solution.py:53
  171.2 34.8 %collective-permute-start.8 = (bf16[256,512]{1,0:T(8,128)(2,1)S(1)}, bf16[256,512]{1,0:T(8,128)(2,1)S(1)}, u32[]{:S(2)}, u32[]{:S(2)}) collective-permute-start(bf16[256,512]{1,0:T(8,128)(2,1)S(1)} %get-tuple-element.20), channel_id=1, source_target_pairs={{0,3},{1,0},{2,1},{3,2},{4,7},{5,4},{6,5},{7,6},{8,11},{9,8},{10,9... | collective-permute-start | bytes 786440 | tf_op jit(solution)/shard_map/ppermute | solution.py:53
  187.4 23.6 %collective-permute-start.10 = (bf16[256,512]{1,0:T(8,128)(2,1)S(1)}, bf16[256,512]{1,0:T(8,128)(2,1)S(1)}, u32[]{:S(2)}, u32[]{:S(2)}) collective-permute-start(bf16[256,512]{1,0:T(8,128)(2,1)S(1)} %get-tuple-element.24), channel_id=1, source_target_pairs={{0,2},{1,3},{2,0},{3,1},{4,6},{5,7},{6,4},{7,5},{8,10},{9,11},{10,... | collective-permute-start | bytes 786440 | tf_op jit(solution)/shard_map/ppermute | solution.py:53
  188.1 22.9 %collective-permute-start.11 = (bf16[256,512]{1,0:T(8,128)(2,1)S(1)}, bf16[256,512]{1,0:T(8,128)(2,1)S(1)}, u32[]{:S(2)}, u32[]{:S(2)}) collective-permute-start(bf16[256,512]{1,0:T(8,128)(2,1)S(1)} %get-tuple-element.23), channel_id=1, source_target_pairs={{0,3},{1,0},{2,1},{3,2},{4,7},{5,4},{6,5},{7,6},{8,11},{9,8},{10,9... | collective-permute-start | bytes 786440 | tf_op jit(solution)/shard_map/ppermute | solution.py:53
  190.4 20.6 %collective-permute-start.9 = (bf16[256,512]{1,0:T(8,128)(2,1)S(1)}, bf16[256,512]{1,0:T(8,128)(2,1)S(1)}, u32[]{:S(2)}, u32[]{:S(2)}) collective-permute-start(bf16[256,512]{1,0:T(8,128)(2,1)S(1)} %get-tuple-element.22), channel_id=1, source_target_pairs={{0,1},{1,2},{2,3},{3,0},{4,5},{5,6},{6,7},{7,4},{8,9},{9,10},{10,1... | collective-permute-start | bytes 786440 | tf_op jit(solution)/shard_map/ppermute | solution.py:53
Sparse Core Ops, SparseCore 0:
  16.5 150.1 all-gather.1

commit v3 on v2

--- a/solution.py
+++ b/solution.py
@@ -58,10 +58,13 @@
     chip_count = lax.axis_size("chip")
     core_index = lax.axis_index("core")
     total_tokens = tokens.shape[0] * chip_count * 2 * lax.axis_size("node")
-    local_weight = dequantized(weight_codes, block_scales)
-    part = local_weight.shape[0] // (chip_count * 2)
+    part = weight_codes.shape[0] // (chip_count * 2)
     place = lax.axis_index("chip") * 2 + core_index
-    piece = lax.dynamic_slice_in_dim(local_weight, place * part, part, 0)
+    block_rows = weight_codes.shape[0] // block_scales.shape[0]
+    piece = dequantized(
+        lax.dynamic_slice_in_dim(weight_codes, place * part, part, 0),
+        lax.dynamic_slice_in_dim(block_scales, place * part // block_rows, max(1, part // block_rows), 0),
+    )
     tokens, value_grad, piece = lax.optimization_barrier((tokens, value_grad, piece))
     full_weight = lax.all_gather(piece, ("node", "chip", "core"), axis=0, tiled=True)
     width = value_grad.shape[1] // CHUNKS

time: 222 us -> 218 us (0.982)
  local copies, waits for them, and re-layouts: 24.2 us -> 18.4 us
  waiting for transfers between devices: 96.3 us -> 98.6 us
    unnamed x16 -> x18, local copies, waits for them, and re-layouts: 15.8 us -> 10.5 us
  transfers between devices with their start and end apart: 13 -> 13, of which waited for: 5 -> 5; matrix products, arithmetic and copies ran while one was open for 33% -> 34% of each run, Pallas kernels for 0% -> 0%
where the time goes in v3:
time: 218 us; the launch traced here: 215 us
  waiting for transfers between devices  98.6 us (45%)
  matrix products  46.5 us (21%)
  other arithmetic  21.3 us (10%)
  local copies, waits for them, and re-layouts  18.4 us (8%)
  starting transfers between devices  15.8 us (7%)
  between operations  14.2 us (7%)
    ppermute x6, waiting for transfers between devices, halved(): came = lax.ppermute(going, axis_name, pairs)  91.7 us
    dot_general x2, matrix products, shards(): lax.dot_general(tokens, value_grad[:, chunk * width:(chunk + 1) * width],...  16.3 us
    dot_general x1, matrix products, shards(): jnp.dot(tokens, full_weight, preferred_element_type=jnp.float32)  15.6 us
    dot_general x1, matrix products, shards(): lax.dot_general(value_grad, full_weight, (((1,), (1,)), ((), ())), prefer...  14.7 us
    convert_element_type x4, other arithmetic, halved(): (kept.astype(jnp.float32) + came.astype(jnp.float32)).astype(jnp.bfloat16)  14.5 us
    unnamed x18, local copies, waits for them, and re-layouts  10.5 us
    ppermute x6, starting transfers between devices, node_sum(): total = total + lax.ppermute(going, 'node', pairs).astype(jnp.float32)  8 us
    ppermute x6, starting transfers between devices, halved(): came = lax.ppermute(going, axis_name, pairs)  7.78 us
  transfers between devices with their start and end apart: 13, of which 5 were waited for; matrix products, arithmetic and copies ran while one was open for 34% of the time, Pallas kernels for 0%

profile of v3, /device:TPU:0, one launch (start us, length us, event | category | flops | bytes accessed | tf_op | source)
XLA Modules:
  0.0 214.9 jit_solution(4984315714849484545)
XLA Ops:
  8.2 2.1 fusion.7
  10.3 8.0 %multiply_convert_fusion = bf16[8192,512]{1,0:T(8,128)(2,1)S(1)} fusion(bf16[512,8192]{1,0:T(8,128)(2,1)} %param.4, bf16[512,1024]{1,0:T(8,128)(2,1)} %param.7), kind=kOutput, calls=%fused_computation | convolution fusion | flops 4303355904 | bytes 17301504 | tf_op jit(solution)/shard_map/dot_general | solution.py:73
  18.3 2.2 %dynamic-slice_bitcast_fusion = bf16[4,1024,512]{2,1,0:T(8,128)(2,1)} fusion(bf16[4,2,1024,512]{3,2,1,0:T(8,128)(2,1)S(1)} %bitcast.76, s32[]{:T(128)S(6)} %select_n.98), kind=kLoop, calls=%fused_computation.11 | loop fusion | bytes 8388612 | tf_op jit(solution)/shard_map/jit(dynamic_index_in_dim)/squeeze | solution.py:22
  20.6 2.6 %copy-done.7 = bf16[8192,512]{1,0:T(8,128)(2,1)} copy-done((bf16[8192,512]{1,0:T(8,128)(2,1)}, bf16[8192,512]{1,0:T(8,128)(2,1)S(1)}, u32[]{:S(2)}) %copy-start.7) | copy-done | bytes 8388632
  23.6 8.2 %multiply_convert_fusion.1 = bf16[8192,512]{1,0:T(8,128)(2,1)S(1)} fusion(bf16[512,8192]{1,0:T(8,128)(2,1)} %param.4, bf16[512,1024]{1,0:T(8,128)(2,1)S(1)} %copy-done.8), kind=kOutput, calls=%fused_computation.1 | convolution fusion | flops 4303355904 | bytes 17301504 | tf_op jit(solution)/shard_map/dot_general | solution.py:73
  31.9 2.5 %dynamic-slice_bitcast_fusion.1 = bf16[4,1024,512]{2,1,0:T(8,128)(2,1)} fusion(bf16[4,2,1024,512]{3,2,1,0:T(8,128)(2,1)S(1)} %bitcast.74, s32[]{:T(128)S(6)} %select_n.98), kind=kLoop, calls=%fused_computation.12 | loop fusion | bytes 8388612 | tf_op jit(solution)/shard_map/jit(dynamic_index_in_dim)/squeeze | solution.py:22
  34.3 2.1 copy-done.6
  36.5 4.7 %fusion = bf16[4,1024,512]{2,1,0:T(8,128)(2,1)S(1)} fusion(bf16[4,1024,512]{2,1,0:T(8,128)(2,1)} %collective-permute-done.3, bf16[4,2,1024,512]{3,2,1,0:T(8,128)(2,1)} %bitcast.77, s32[]{:T(128)S(6)} %select_n.97), kind=kLoop, calls=%fused_computation.4 | loop fusion | flops 8388608 | bytes 12582916 | tf_op jit(solution)/shard_map/convert_element_type | solution.py:25
  41.2 2.0 copy-done.2
  43.4 3.1 %collective-permute-start.4 = (bf16[1,2048,512]{2,1,0:T(8,128)(2,1)S(1)}, bf16[1,2048,512]{2,1,0:T(8,128)(2,1)}, u32[]{:S(2)}, u32[]{:S(2)}) collective-permute-start(bf16[1,2048,512]{2,1,0:T(8,128)(2,1)S(1)} %dynamic-slice_bitcast_fusion.2), channel_id=1, source_target_pairs={{0,16},{8,24},{16,0},{24,8},{1,17},{9,25},{17,1},{25,9},{2,18},{10... | collective-permute-start | bytes 6291464 | tf_op jit(solution)/shard_map/ppermute | solution.py:24
  46.5 4.7 %fusion.1 = bf16[4,1024,512]{2,1,0:T(8,128)(2,1)S(1)} fusion(bf16[4,1024,512]{2,1,0:T(8,128)(2,1)} %collective-permute-done, bf16[4,2,1024,512]{3,2,1,0:T(8,128)(2,1)} %bitcast.75, s32[]{:T(128)S(6)} %select_n.97), kind=kLoop, calls=%fused_computation.6 | loop fusion | flops 8388608 | bytes 12582916 | tf_op jit(solution)/shard_map/convert_element_type | solution.py:25
  51.2 1.9 copy-done.3
  56.1 59.0 %collective-permute-done.4 = bf16[1,2048,512]{2,1,0:T(8,128)(2,1)} collective-permute-done((bf16[1,2048,512]{2,1,0:T(8,128)(2,1)S(1)}, bf16[1,2048,512]{2,1,0:T(8,128)(2,1)}, u32[]{:S(2)}, u32[]{:S(2)}) %collective-permute-start.4) | collective-permute-done | bytes 2097184 | tf_op jit(solution)/shard_map/ppermute | solution.py:24
  115.1 2.8 %fusion.2 = bf16[1,2048,512]{2,1,0:T(8,128)(2,1)S(1)} fusion(bf16[1,2048,512]{2,1,0:T(8,128)(2,1)} %collective-permute-done.4, bf16[1,2,2048,512]{3,2,1,0:T(8,128)(2,1)} %bitcast.69, s32[]{:T(128)S(6)} %select_n.104), kind=kLoop, calls=%fused_computation.8 | loop fusion | flops 4194304 | bytes 6291460 | tf_op jit(solution)/shard_map/convert_element_type | solution.py:25
  118.0 1.6 collective-permute-start.5
  119.6 11.0 %collective-permute-done.1 = bf16[2,1024,512]{2,1,0:T(8,128)(2,1)} collective-permute-done((bf16[2,1024,512]{2,1,0:T(8,128)(2,1)}, bf16[2,1024,512]{2,1,0:T(8,128)(2,1)}, u32[]{:S(2)}, u32[]{:S(2)}) %collective-permute-start.1) | collective-permute-done | bytes 2097184 | tf_op jit(solution)/shard_map/ppermute | solution.py:24
  130.6 2.3 %fusion.3 = bf16[2,1024,512]{2,1,0:T(8,128)(2,1)S(1)} fusion(bf16[2,1024,512]{2,1,0:T(8,128)(2,1)} %collective-permute-done.1, bf16[2,2,1024,512]{3,2,1,0:T(8,128)(2,1)S(1)} %bitcast.71, s32[]{:T(128)S(6)} %select_n.100), kind=kLoop, calls=%fused_computation.10 | loop fusion | flops 4194304 | bytes 6291460 | tf_op jit(solution)/shard_map/convert_element_type | solution.py:25
  136.2 21.8 %collective-permute-done.5 = bf16[1,1024,512]{2,1,0:T(8,128)(2,1)} collective-permute-done((bf16[1,1024,512]{2,1,0:T(8,128)(2,1)S(1)}, bf16[1,1024,512]{2,1,0:T(8,128)(2,1)}, u32[]{:S(2)}, u32[]{:S(2)}) %collective-permute-start.5) | collective-permute-done | bytes 1048608 | tf_op jit(solution)/shard_map/ppermute | solution.py:24
  159.6 1.8 fusion.5
  163.1 2.4 %collective-permute-start.7 = (bf16[256,512]{1,0:T(8,128)(2,1)S(1)}, bf16[256,512]{1,0:T(8,128)(2,1)S(1)}, u32[]{:S(2)}, u32[]{:S(2)}) collective-permute-start(bf16[256,512]{1,0:T(8,128)(2,1)S(1)} %get-tuple-element.21), channel_id=1, source_target_pairs={{0,2},{1,3},{2,0},{3,1},{4,6},{5,7},{6,4},{7,5},{8,10},{9,11},{10,... | collective-permute-start | bytes 786440 | tf_op jit(solution)/shard_map/ppermute | solution.py:53
  165.5 1.9 collective-permute-start.8
  167.3 14.7 %convolution_convert_fusion = bf16[512,8192]{1,0:T(8,128)(2,1)} fusion(bf16[512,1024]{1,0:T(8,128)(2,1)} %param.7, bf16[8192,1024]{1,0:T(8,128)(2,1)} %all-gather.2.cloned.1.call-done), kind=kOutput, calls=%fused_computation.2 | convolution fusion | flops 8594128896 | bytes 26214400 | tf_op jit(solution)/shard_map/dot_general | solution.py:81
  185.6 15.6 %convolution_convert_fusion.1 = bf16[512,1024]{1,0:T(8,128)(2,1)} fusion(bf16[512,8192]{1,0:T(8,128)(2,1)} %param.4, bf16[8192,1024]{1,0:T(8,128)(2,1)} %all-gather.2.cloned.1.call-done), kind=kOutput, calls=%fused_computation.18 | convolution fusion | flops 8590458880 | bytes 26214400 | tf_op jit(solution)/shard_map/dot_general | solution.py:85
  201.4 5.5 %collective-permute-done.10 = bf16[256,512]{1,0:T(8,128)(2,1)S(1)} collective-permute-done((bf16[256,512]{1,0:T(8,128)(2,1)S(1)}, bf16[256,512]{1,0:T(8,128)(2,1)S(1)}, u32[]{:S(2)}, u32[]{:S(2)}) %collective-permute-start.10) | collective-permute-done | bytes 262176 | tf_op jit(solution)/shard_map/ppermute | solution.py:53
  (46 shorter events, 16.3 us)
Async XLA Ops:
  7.2 0.7 copy-start
  7.2 155.6 %all-gather.2.cloned.1.call-start = ((), (), s32[]{:S(2)}) async-start(), calls=%async_computation | async-start | bytes 17301504 | tf_op jit(solution)/shard_map/all_gather | solution.py:69
  18.3 4.8 %copy-start.7 = (bf16[8192,512]{1,0:T(8,128)(2,1)}, bf16[8192,512]{1,0:T(8,128)(2,1)S(1)}, u32[]{:S(2)}) copy-start(bf16[8192,512]{1,0:T(8,128)(2,1)S(1)} %multiply_convert_fusion) | copy-start | bytes 25165828
  18.3 5.3 %copy-start.8 = (bf16[512,1024]{1,0:T(8,128)(2,1)S(1)}, bf16[512,1024]{1,0:T(8,128)(2,1)}, u32[]{:S(2)}) copy-start(bf16[512,1024]{1,0:T(8,128)(2,1)} %param.7) | copy-start | bytes 3145732
  23.1 13.4 %collective-permute-start.3 = (bf16[4,1024,512]{2,1,0:T(8,128)(2,1)}, bf16[4,1024,512]{2,1,0:T(8,128)(2,1)}, u32[]{:S(2)}, u32[]{:S(2)}) collective-permute-start(bf16[4,1024,512]{2,1,0:T(8,128)(2,1)} %dynamic-slice_bitcast_fusion), channel_id=1, source_target_pairs={{0,4},{4,0},{1,5},{5,1},{2,6},{6,2},{3,7},{7,3},{8,12},{12,8},{9,1... | collective-permute-start | bytes 12582920 | tf_op jit(solution)/shard_map/ppermute | solution.py:24
  31.9 4.5 %copy-start.6 = (bf16[8192,512]{1,0:T(8,128)(2,1)}, bf16[8192,512]{1,0:T(8,128)(2,1)S(1)}, u32[]{:S(2)}) copy-start(bf16[8192,512]{1,0:T(8,128)(2,1)S(1)} %multiply_convert_fusion.1) | copy-start | bytes 25165828
  36.4 10.1 %collective-permute-start = (bf16[4,1024,512]{2,1,0:T(8,128)(2,1)}, bf16[4,1024,512]{2,1,0:T(8,128)(2,1)}, u32[]{:S(2)}, u32[]{:S(2)}) collective-permute-start(bf16[4,1024,512]{2,1,0:T(8,128)(2,1)} %dynamic-slice_bitcast_fusion.1), channel_id=1, source_target_pairs={{0,4},{4,0},{1,5},{5,1},{2,6},{6,2},{3,7},{7,3},{8,12},{12,8},{9,1... | collective-permute-start | bytes 12582920 | tf_op jit(solution)/shard_map/ppermute | solution.py:24
  41.2 2.0 copy-start.2
  43.4 71.8 %collective-permute-start.4 = (bf16[1,2048,512]{2,1,0:T(8,128)(2,1)S(1)}, bf16[1,2048,512]{2,1,0:T(8,128)(2,1)}, u32[]{:S(2)}, u32[]{:S(2)}) collective-permute-start(bf16[1,2048,512]{2,1,0:T(8,128)(2,1)S(1)} %dynamic-slice_bitcast_fusion.2), channel_id=1, source_target_pairs={{0,16},{8,24},{16,0},{24,8},{1,17},{9,25},{17,1},{25,9},{2,18},{10... | collective-permute-start | bytes 6291464 | tf_op jit(solution)/shard_map/ppermute | solution.py:24
  51.2 1.9 copy-start.3
  54.7 75.9 %collective-permute-start.1 = (bf16[2,1024,512]{2,1,0:T(8,128)(2,1)}, bf16[2,1024,512]{2,1,0:T(8,128)(2,1)}, u32[]{:S(2)}, u32[]{:S(2)}) collective-permute-start(bf16[2,1024,512]{2,1,0:T(8,128)(2,1)} %dynamic-slice_bitcast_fusion.3), channel_id=1, source_target_pairs={{0,8},{8,0},{16,24},{24,16},{1,9},{9,1},{17,25},{25,17},{2,10},{10... | collective-permute-start | bytes 6291464 | tf_op jit(solution)/shard_map/ppermute | solution.py:24
  56.1 74.5 %copy-start.4 = (bf16[4,1024,512]{2,1,0:T(8,128)(2,1)S(1)}, bf16[4,1024,512]{2,1,0:T(8,128)(2,1)}, u32[]{:S(2)}) copy-start(bf16[4,1024,512]{2,1,0:T(8,128)(2,1)} %copy-done.3) | copy-start | bytes 12582916
  118.0 40.0 %collective-permute-start.5 = (bf16[1,1024,512]{2,1,0:T(8,128)(2,1)S(1)}, bf16[1,1024,512]{2,1,0:T(8,128)(2,1)}, u32[]{:S(2)}, u32[]{:S(2)}) collective-permute-start(bf16[1,1024,512]{2,1,0:T(8,128)(2,1)S(1)} %dynamic-slice_bitcast_fusion.4), channel_id=1, source_target_pairs={{0,8},{8,0},{16,24},{24,16},{1,9},{9,1},{17,25},{25,17},{2,10},{10... | collective-permute-start | bytes 3145736 | tf_op jit(solution)/shard_map/ppermute | solution.py:24
  132.9 1.3 copy-start.5
  135.2 24.4 %collective-permute-start.2 = (bf16[1,1024,512]{2,1,0:T(8,128)(2,1)}, bf16[1,1024,512]{2,1,0:T(8,128)(2,1)}, u32[]{:S(2)}, u32[]{:S(2)}) collective-permute-start(bf16[1,1024,512]{2,1,0:T(8,128)(2,1)} %constant_dynamic-slice_fusion), channel_id=1, source_target_pairs={{0,16},{8,24},{16,0},{24,8},{1,17},{9,25},{17,1},{25,9},{2,18},{10... | collective-permute-start | bytes 3145736 | tf_op jit(solution)/shard_map/ppermute | solution.py:24
  162.9 21.8 %collective-permute-start.6 = (bf16[256,512]{1,0:T(8,128)(2,1)S(1)}, bf16[256,512]{1,0:T(8,128)(2,1)S(1)}, u32[]{:S(2)}, u32[]{:S(2)}) collective-permute-start(bf16[256,512]{1,0:T(8,128)(2,1)S(1)} %get-tuple-element.19), channel_id=1, source_target_pairs={{0,1},{1,2},{2,3},{3,0},{4,5},{5,6},{6,7},{7,4},{8,9},{9,10},{10,1... | collective-permute-start | bytes 786440 | tf_op jit(solution)/shard_map/ppermute | solution.py:53
  163.1 38.2 %collective-permute-start.7 = (bf16[256,512]{1,0:T(8,128)(2,1)S(1)}, bf16[256,512]{1,0:T(8,128)(2,1)S(1)}, u32[]{:S(2)}, u32[]{:S(2)}) collective-permute-start(bf16[256,512]{1,0:T(8,128)(2,1)S(1)} %get-tuple-element.21), channel_id=1, source_target_pairs={{0,2},{1,3},{2,0},{3,1},{4,6},{5,7},{6,4},{7,5},{8,10},{9,11},{10,... | collective-permute-start | bytes 786440 | tf_op jit(solution)/shard_map/ppermute | solution.py:53
  165.5 35.8 %collective-permute-start.8 = (bf16[256,512]{1,0:T(8,128)(2,1)S(1)}, bf16[256,512]{1,0:T(8,128)(2,1)S(1)}, u32[]{:S(2)}, u32[]{:S(2)}) collective-permute-start(bf16[256,512]{1,0:T(8,128)(2,1)S(1)} %get-tuple-element.20), channel_id=1, source_target_pairs={{0,3},{1,0},{2,1},{3,2},{4,7},{5,4},{6,5},{7,6},{8,11},{9,8},{10,9... | collective-permute-start | bytes 786440 | tf_op jit(solution)/shard_map/ppermute | solution.py:53
  182.1 24.7 %collective-permute-start.10 = (bf16[256,512]{1,0:T(8,128)(2,1)S(1)}, bf16[256,512]{1,0:T(8,128)(2,1)S(1)}, u32[]{:S(2)}, u32[]{:S(2)}) collective-permute-start(bf16[256,512]{1,0:T(8,128)(2,1)S(1)} %get-tuple-element.24), channel_id=1, source_target_pairs={{0,2},{1,3},{2,0},{3,1},{4,6},{5,7},{6,4},{7,5},{8,10},{9,11},{10,... | collective-permute-start | bytes 786440 | tf_op jit(solution)/shard_map/ppermute | solution.py:53
  183.6 23.2 %collective-permute-start.11 = (bf16[256,512]{1,0:T(8,128)(2,1)S(1)}, bf16[256,512]{1,0:T(8,128)(2,1)S(1)}, u32[]{:S(2)}, u32[]{:S(2)}) collective-permute-start(bf16[256,512]{1,0:T(8,128)(2,1)S(1)} %get-tuple-element.23), channel_id=1, source_target_pairs={{0,3},{1,0},{2,1},{3,2},{4,7},{5,4},{6,5},{7,6},{8,11},{9,8},{10,9... | collective-permute-start | bytes 786440 | tf_op jit(solution)/shard_map/ppermute | solution.py:53
  184.7 22.2 %collective-permute-start.9 = (bf16[256,512]{1,0:T(8,128)(2,1)S(1)}, bf16[256,512]{1,0:T(8,128)(2,1)S(1)}, u32[]{:S(2)}, u32[]{:S(2)}) collective-permute-start(bf16[256,512]{1,0:T(8,128)(2,1)S(1)} %get-tuple-element.22), channel_id=1, source_target_pairs={{0,1},{1,2},{2,3},{3,0},{4,5},{5,6},{6,7},{7,4},{8,9},{9,10},{10,1... | collective-permute-start | bytes 786440 | tf_op jit(solution)/shard_map/ppermute | solution.py:53
  185.6 22.4 %copy-start.1 = (f32[16,8]{0,1:T(8,128)S(1)}, f32[16,8]{0,1:T(8,128)}, u32[]{:S(2)}) copy-start(f32[16,8]{0,1:T(8,128)} %param.6) | copy-start | bytes 1540
Sparse Core Ops, SparseCore 0:
  11.4 151.3 all-gather.1
